TPU v7x, 32 devices: a whole 2x2x4 slice. The times are simulated.
32 devices in a mesh: fsdp: 2 (over core), context: 8 (over z, x), tensor: 2 (over y).
Axes of the slice: x: 2, y: 2, z: 4, core: 2. Of those that a mesh axis runs over, the one named last changes fastest.
Arguments:
- tokens: bfloat16 [8192, 1024], P(('fsdp', 'context')), may hold values from -6 to 6
- doc_blocks: int32 [2, 3], P('fsdp'), may hold values from 8 to 16, as said below
- pad_tokens: int32 [2, 3], P('fsdp'), may hold values from 0 to 127
- w_qkv: bfloat16 [1024, 3, 1024], P(('fsdp', 'context'), None, 'tensor'), may hold values from -0.25 to 0.25
- bias_query: float32 [1024], P('tensor'), may hold values from -3 to 3
- bias_value: float32 [1024], P('tensor'), may hold values from -3 to 3
- w_attn_out: bfloat16 [1024, 1024], P('tensor', ('fsdp', 'context')), may hold values from -1 to 1
- bias_attn_out: float32 [1024], replicated, may hold values from -3 to 3
- gain_one: float32 [1024], replicated, may hold values from 0.5 to 1.5
- shift_one: float32 [1024], replicated, may hold values from -3 to 3
- w_up: bfloat16 [1024, 4096], P(('fsdp', 'context'), 'tensor'), may hold values from -0.1875 to 0.1875
- bias_up: float32 [4096], P('tensor'), may hold values from -3 to 3
- w_down: bfloat16 [4096, 1024], P('tensor', ('fsdp', 'context')), may hold values from -0.125 to 0.125
- bias_down: float32 [1024], replicated, may hold values from -3 to 3
- gain_two: float32 [1024], replicated, may hold values from 0.5 to 1.5
- shift_two: float32 [1024], replicated, may hold values from -3 to 3
- cotangent: bfloat16 [8192, 1024], P(('fsdp', 'context')), may hold values from -6 to 6
Outputs:
- output: bfloat16 [8192, 1024], P(('fsdp', 'context'))
- grad_tokens: float32 [8192, 1024], P(('fsdp', 'context'))
- grad_w_qkv: float32 [1024, 3, 1024], P(('fsdp', 'context'), None, 'tensor')
- grad_bias_query: float32 [1024], P('tensor')
- grad_bias_value: float32 [1024], P('tensor')
- grad_w_attn_out: float32 [1024, 1024], P('tensor', ('fsdp', 'context'))
- grad_bias_attn_out: float32 [1024], replicated
- grad_gain_one: float32 [1024], replicated
- grad_shift_one: float32 [1024], replicated
- grad_w_up: float32 [1024, 4096], P(('fsdp', 'context'), 'tensor')
- grad_bias_up: float32 [4096], P('tensor')
- grad_w_down: float32 [4096, 1024], P('tensor', ('fsdp', 'context'))
- grad_bias_down: float32 [1024], replicated
- grad_gain_two: float32 [1024], replicated
- grad_shift_two: float32 [1024], replicated
Inputs may be any that keep to these rules, and one draw needn't show every extreme that they name: `doc_blocks`: each row sums to 32; its largest entry is exactly 16.
All inputs are finite; a program needn't handle non-finite values.
Results may differ from a plain program's by a relative error of at most 0.028.
Values may be sent and summed in bfloat16 or wider, within the bound.
A program may use at most 192 MiB of HBM per device.

v0:
```python
import jax
import jax.numpy as jnp
from jax import lax
from jax.sharding import PartitionSpec as P

HEAD = 64
TOK_DEV = 512
BLK = 128
MAXB = 16
QB = 512


EPSILON = 1e-05
MASKED = -1e30


def block_place(stored, contexts):
    local_row = stored % TOK_DEV
    owner = stored // TOK_DEV
    return (local_row // BLK * contexts + owner) * BLK + local_row % BLK


def doc_of(doc_row, pad_row, positions):
    doc_ends = jnp.cumsum(doc_row) * BLK
    doc_index = jnp.sum((positions[:, None] >= doc_ends[None, :]).astype(jnp.int32), axis=1)
    chosen = doc_index[:, None] == jnp.arange(doc_ends.shape[0], dtype=jnp.int32)[None, :]
    live_end = jnp.sum(jnp.where(chosen, doc_ends - pad_row, 0), axis=1)
    return (doc_index, positions < live_end)


def layer_norm(hidden, gain_vec, bias_add):
    row_mean = jnp.mean(hidden, axis=-1, keepdims=True)
    centred = hidden - row_mean
    factor = lax.rsqrt(jnp.mean(centred * centred, axis=-1, keepdims=True) + EPSILON)
    normed = centred * factor
    return (normed * gain_vec + bias_add, normed, factor)


def norm_back(grad_in, normed, factor, gain_vec):
    scaled = grad_in * gain_vec
    return factor * (
        scaled
        - jnp.mean(scaled, axis=-1, keepdims=True)
        - normed * jnp.mean(scaled * normed, axis=-1, keepdims=True)
    )


def per_device(
    tokens,
    doc_blocks,
    pad_tokens,
    w_qkv,
    bias_query,
    bias_value,
    w_attn_out,
    bias_attn_out,
    gain_one,
    shift_one,
    w_up,
    bias_up,
    w_down,
    bias_down,
    gain_two,
    shift_two,
    cotangent,
):
    contexts = lax.axis_size("context")
    row_count = tokens.shape[0]
    share_rows = row_count // lax.axis_size("tensor")
    share_start = lax.axis_index("tensor") * share_rows
    slots = row_count // BLK
    group_rows = row_count * contexts
    window = MAXB * BLK
    per_step = QB // BLK
    step_count = slots // per_step
    start_here = lax.axis_index("context") * row_count
    doc_row = doc_blocks[0]
    pad_row = pad_tokens[0]
    doc_ends = jnp.cumsum(doc_row) * BLK
    doc_starts = doc_ends - doc_row * BLK
    own_places = block_place(start_here + jnp.arange(row_count, dtype=jnp.int32), contexts)
    own_doc, own_live = doc_of(doc_row, pad_row, own_places)
    slot_first = own_places.reshape(slots, BLK)[:, 0]
    slot_doc = jnp.sum((slot_first[:, None] >= doc_ends[None, :]).astype(jnp.int32), axis=1)
    chosen = slot_doc[:, None] == jnp.arange(doc_ends.shape[0], dtype=jnp.int32)[None, :]
    own_begin = jnp.minimum(
        jnp.sum(jnp.where(chosen, doc_starts[None, :], 0), axis=1), group_rows - window
    )
    window_places = (own_begin[:, None] + jnp.arange(window, dtype=jnp.int32)[None, :]).reshape(-1)
    win_doc, win_live = doc_of(doc_row, pad_row, window_places)
    win_doc = win_doc.reshape(slots, window)
    win_live = win_live.reshape(slots, window)
    own_doc_slots = own_doc.reshape(slots, BLK)

    def position_order(gathered):
        rest = gathered.shape[1:]
        return jnp.swapaxes(gathered.reshape((contexts, slots, BLK) + rest), 0, 1).reshape(
            (group_rows,) + rest
        )

    def windows(source, begins):
        return jax.vmap(lambda begin: lax.dynamic_slice_in_dim(source, begin, window, 0))(begins)

    full_qkv, full_out, full_up, full_down = (
        lax.all_gather(w_qkv, ("fsdp", "context"), axis=0, tiled=True),
        lax.all_gather(w_attn_out, ("fsdp", "context"), axis=1, tiled=True),
        lax.all_gather(w_up, ("fsdp", "context"), axis=0, tiled=True),
        lax.all_gather(w_down, ("fsdp", "context"), axis=1, tiled=True),
    )
    inner_width = w_qkv.shape[2]
    heads_here = inner_width // HEAD
    score_scale = HEAD ** (-0.5)
    head_shape = (row_count, heads_here, HEAD)
    slot_shape = (slots, BLK, heads_here, HEAD)
    bias_three = jnp.stack([bias_query, jnp.zeros_like(bias_query), bias_value])
    qkv_low = (
        jnp.einsum("td,dce->tce", tokens, full_qkv, preferred_element_type=jnp.float32) + bias_three
    ).astype(jnp.bfloat16)
    query_low = qkv_low[:, 0].reshape(head_shape)
    key_low = qkv_low[:, 1].reshape(head_shape)
    value_low = qkv_low[:, 2].reshape(head_shape)
    query_slots = query_low.reshape(slot_shape)
    key_all, value_all = (
        lax.all_gather(key_low, "context", axis=0, tiled=True),
        lax.all_gather(value_low, "context", axis=0, tiled=True),
    )
    key_pos = position_order(key_all)
    value_pos = position_order(value_all)

    def slot_scores(query_part, key_part, query_doc, key_doc, key_live):
        raw = (
            jnp.einsum("sqhd,skhd->sqhk", query_part, key_part, preferred_element_type=jnp.float32)
            * score_scale
        )
        allowed = ((query_doc[:, :, None] == key_doc[:, None, :]) & key_live[:, None, :])[
            :, :, None, :
        ]
        return (jnp.where(allowed, raw, MASKED), allowed)

    def forward_step(step):
        key_part = windows(key_pos, own_begin)
        value_part = windows(value_pos, own_begin)
        scores, allowed = slot_scores(query_slots, key_part, own_doc_slots, win_doc, win_live)
        top = jnp.max(scores, axis=3)
        total = jnp.sum(jnp.where(allowed, jnp.exp(scores - top[:, :, :, None]), 0.0), axis=3)
        log_part = top + jnp.log(total)
        prob_low = jnp.where(allowed, jnp.exp(scores - log_part[:, :, :, None]), 0.0).astype(
            jnp.bfloat16
        )
        return (
            jnp.einsum("sqhk,skhd->sqhd", prob_low, value_part, preferred_element_type=jnp.float32),
            log_part,
        )

    attended_steps, log_steps = lax.map(forward_step, jnp.arange(step_count, dtype=jnp.int32))
    attended = attended_steps.reshape(head_shape)
    log_total = log_steps.reshape(row_count, heads_here)
    attended_low = attended.reshape(row_count, inner_width).astype(jnp.bfloat16)
    branch_share = (
        lax.psum_scatter(
            jnp.dot(attended_low, full_out, preferred_element_type=jnp.float32).astype(
                jnp.bfloat16
            ),
            "tensor",
            scatter_dimension=0,
            tiled=True,
        ).astype(jnp.float32)
        + bias_attn_out
    )
    token_share = lax.dynamic_slice_in_dim(tokens, share_start, share_rows, 0).astype(jnp.float32)
    first_share, normed_one_share, factor_one_share = layer_norm(
        token_share + branch_share, gain_one, shift_one
    )
    first, normed_one, factor_one = (
        lax.all_gather(first_share.astype(jnp.bfloat16), "tensor", axis=0, tiled=True).astype(
            first_share.dtype
        ),
        lax.all_gather(normed_one_share.astype(jnp.bfloat16), "tensor", axis=0, tiled=True).astype(
            normed_one_share.dtype
        ),
        lax.all_gather(factor_one_share.astype(jnp.bfloat16), "tensor", axis=0, tiled=True).astype(
            factor_one_share.dtype
        ),
    )
    first_low = first.astype(jnp.bfloat16)
    pre = jnp.dot(first_low, full_up, preferred_element_type=jnp.float32) + bias_up
    act, gelu_back = jax.vjp(lambda hidden: jax.nn.gelu(hidden, approximate=False), pre)
    act_low = act.astype(jnp.bfloat16)
    feed_share = (
        lax.psum_scatter(
            jnp.dot(act_low, full_down, preferred_element_type=jnp.float32).astype(jnp.bfloat16),
            "tensor",
            scatter_dimension=0,
            tiled=True,
        ).astype(jnp.float32)
        + bias_down
    )
    out_share, normed_two_share, factor_two_share = layer_norm(
        first_share + feed_share, gain_two, shift_two
    )
    result_out, normed_two, factor_two = (
        lax.all_gather(out_share.astype(jnp.bfloat16), "tensor", axis=0, tiled=True).astype(
            out_share.dtype
        ),
        lax.all_gather(normed_two_share.astype(jnp.bfloat16), "tensor", axis=0, tiled=True).astype(
            normed_two_share.dtype
        ),
        lax.all_gather(factor_two_share.astype(jnp.bfloat16), "tensor", axis=0, tiled=True).astype(
            factor_two_share.dtype
        ),
    )
    output = result_out.astype(jnp.bfloat16)
    grad_out = cotangent.astype(jnp.float32)
    grad_gain_two = jnp.sum(grad_out * normed_two, axis=0)
    grad_shift_two = jnp.sum(grad_out, axis=0)
    grad_second = norm_back(grad_out, normed_two, factor_two, gain_two)
    grad_feed = grad_second.astype(jnp.bfloat16)
    grad_bias_down = jnp.sum(grad_feed.astype(jnp.float32), axis=0)
    grad_w_down = jnp.einsum("tf,td->fd", act_low, grad_feed, preferred_element_type=jnp.float32)
    grad_act = jnp.einsum("td,fd->tf", grad_feed, full_down, preferred_element_type=jnp.float32)
    grad_pre = gelu_back(grad_act)[0].astype(jnp.bfloat16)
    grad_bias_up = jnp.sum(grad_pre.astype(jnp.float32), axis=0)
    grad_w_up = jnp.einsum("td,tf->df", first_low, grad_pre, preferred_element_type=jnp.float32)
    grad_first = grad_second + lax.psum(
        jnp.einsum("tf,df->td", grad_pre, full_up, preferred_element_type=jnp.float32).astype(
            jnp.bfloat16
        ),
        "tensor",
    ).astype(jnp.float32)
    grad_gain_one = jnp.sum(grad_first * normed_one, axis=0)
    grad_shift_one = jnp.sum(grad_first, axis=0)
    grad_mid = norm_back(grad_first, normed_one, factor_one, gain_one)
    grad_branch = grad_mid.astype(jnp.bfloat16)
    grad_bias_attn_out = jnp.sum(grad_branch.astype(jnp.float32), axis=0)
    grad_w_attn_out = jnp.einsum(
        "te,td->ed", attended_low, grad_branch, preferred_element_type=jnp.float32
    )
    grad_att = (
        jnp.einsum("td,ed->te", grad_branch, full_out, preferred_element_type=jnp.float32)
        .astype(jnp.bfloat16)
        .reshape(head_shape)
    )
    row_delta = jnp.sum(grad_att.astype(jnp.float32) * attended, axis=2)
    grad_slots = grad_att.reshape(slot_shape)
    delta_slots = row_delta.reshape(slots, BLK, heads_here)
    log_slots = log_total.reshape(slots, BLK, heads_here)

    def pair_terms(
        query_part,
        grad_part,
        query_doc,
        query_log,
        query_delta,
        key_part,
        value_part,
        key_doc,
        key_live,
    ):
        scores, allowed = slot_scores(query_part, key_part, query_doc, key_doc, key_live)
        prob = jnp.where(allowed, jnp.exp(scores - query_log[:, :, :, None]), 0.0)
        grad_prob = jnp.einsum(
            "sqhd,skhd->sqhk", grad_part, value_part, preferred_element_type=jnp.float32
        )
        grad_score = (prob * (grad_prob - query_delta[:, :, :, None])).astype(jnp.bfloat16)
        return (prob.astype(jnp.bfloat16), grad_score)

    def query_side():
        key_part = windows(key_pos, own_begin)
        value_part = windows(value_pos, own_begin)
        prob_low, grad_score = pair_terms(
            query_slots,
            grad_slots,
            own_doc_slots,
            log_slots,
            delta_slots,
            key_part,
            value_part,
            win_doc,
            win_live,
        )
        grad_query = (
            jnp.einsum("sqhk,skhd->sqhd", grad_score, key_part, preferred_element_type=jnp.float32)
            * score_scale
        )
        return (own_begin, query_slots, grad_slots, prob_low, grad_score, grad_query)

    def back_step(key_terms, step):
        begins, query_part, grad_part, prob_low, grad_score, grad_query = query_side()
        grad_key = (
            jnp.einsum(
                "sqhk,sqhd->skhd", grad_score, query_part, preferred_element_type=jnp.float32
            )
            * score_scale
        )
        grad_value = jnp.einsum(
            "sqhk,sqhd->skhd", prob_low, grad_part, preferred_element_type=jnp.float32
        )
        terms = jnp.stack([grad_key, grad_value], axis=2)
        for index in range(per_step):
            earlier = lax.dynamic_slice_in_dim(key_terms, begins[index], window, 0)
            key_terms = lax.dynamic_update_slice_in_dim(
                key_terms, earlier + terms[index], begins[index], 0
            )
        return (key_terms, grad_query)

    empty_terms = jnp.zeros((group_rows, 2, heads_here, HEAD), jnp.float32)
    key_terms, query_steps = lax.scan(
        back_step, empty_terms, jnp.arange(step_count, dtype=jnp.int32)
    )
    grad_query = query_steps.reshape(head_shape)
    rest = key_terms.shape[1:]
    own_terms = lax.psum_scatter(
        jnp.swapaxes(key_terms.reshape((slots, contexts, BLK) + rest), 0, 1)
        .reshape((group_rows,) + rest)
        .astype(jnp.bfloat16),
        "context",
        scatter_dimension=0,
        tiled=True,
    ).astype(jnp.float32)
    grad_key = own_terms[:, 0]
    grad_value = own_terms[:, 1]
    grad_qkv = (
        jnp.stack([grad_query, grad_key, grad_value], axis=1)
        .reshape(row_count, 3, inner_width)
        .astype(jnp.bfloat16)
    )
    grad_bias_query = jnp.sum(grad_qkv[:, 0].astype(jnp.float32), axis=0)
    grad_bias_value = jnp.sum(grad_qkv[:, 2].astype(jnp.float32), axis=0)
    grad_w_qkv = jnp.einsum("td,tce->dce", tokens, grad_qkv, preferred_element_type=jnp.float32)
    grad_tokens = grad_mid + lax.psum(
        jnp.einsum("tce,dce->td", grad_qkv, full_qkv, preferred_element_type=jnp.float32).astype(
            jnp.bfloat16
        ),
        "tensor",
    ).astype(jnp.float32)
    shard_qkv, shard_out, shard_up, shard_down = (
        lax.psum_scatter(
            grad_w_qkv.astype(jnp.bfloat16), ("fsdp", "context"), scatter_dimension=0, tiled=True
        ).astype(jnp.float32),
        lax.psum_scatter(
            grad_w_attn_out.astype(jnp.bfloat16),
            ("fsdp", "context"),
            scatter_dimension=1,
            tiled=True,
        ).astype(jnp.float32),
        lax.psum_scatter(
            grad_w_up.astype(jnp.bfloat16), ("fsdp", "context"), scatter_dimension=0, tiled=True
        ).astype(jnp.float32),
        lax.psum_scatter(
            grad_w_down.astype(jnp.bfloat16), ("fsdp", "context"), scatter_dimension=1, tiled=True
        ).astype(jnp.float32),
    )
    small_sums = lax.psum(
        (
            grad_bias_query,
            grad_bias_value,
            grad_bias_attn_out,
            grad_gain_one,
            grad_shift_one,
            grad_bias_up,
            grad_bias_down,
            grad_gain_two,
            grad_shift_two,
        ),
        ("fsdp", "context"),
    )
    return (
        output,
        grad_tokens,
        shard_qkv,
        small_sums[0],
        small_sums[1],
        shard_out,
        small_sums[2],
        small_sums[3],
        small_sums[4],
        shard_up,
        small_sums[5],
        shard_down,
        small_sums[6],
        small_sums[7],
        small_sums[8],
    )


def solution(mesh):
    in_specs = (
        P(("fsdp", "context"), None),
        P("fsdp", None),
        P("fsdp", None),
        P(("fsdp", "context"), None, "tensor"),
        P("tensor"),
        P("tensor"),
        P("tensor", ("fsdp", "context")),
        P(),
        P(),
        P(),
        P(("fsdp", "context"), "tensor"),
        P("tensor"),
        P("tensor", ("fsdp", "context")),
        P(),
        P(),
        P(),
        P(("fsdp", "context"), None),
    )
    out_specs = (
        P(("fsdp", "context"), None),
        P(("fsdp", "context"), None),
        P(("fsdp", "context"), None, "tensor"),
        P("tensor"),
        P("tensor"),
        P("tensor", ("fsdp", "context")),
        P(),
        P(),
        P(),
        P(("fsdp", "context"), "tensor"),
        P("tensor"),
        P("tensor", ("fsdp", "context")),
        P(),
        P(),
        P(),
    )
    return jax.shard_map(
        per_device, mesh=mesh, in_specs=in_specs, out_specs=out_specs, check_vma=False
    )
```

profile of v0, /device:TPU:0, one launch (start us, length us, event | category | flops | bytes accessed | tf_op | source)
XLA Modules:
  0.0 1488.8 jit_solution(12028455730810836610)
XLA Ops:
  8.8 49.4 %all-gather.15.cloned.1.call-done = bf16[1024,3,512]{2,0,1:T(8,128)(2,1)} async-done(((bf16[64,3,512]{2,0,1:T(8,128)(2,1)}), bf16[1024,3,512]{2,0,1:T(8,128)(2,1)}) %all-gather.15.cloned.1.call-update) | async-done | bytes 3145744 | tf_op jit(solution)/shard_map/all_gather | solution.py:105
  58.2 4.1 add_convert_fusion.1
  70.6 66.7 %all-gather.17.cloned.1.call-done = bf16[4096,8,64]{0,2,1:T(8,128)(2,1)} async-done(((bf16[512,8,64]{0,2,1:T(8,128)(2,1)}), bf16[4096,8,64]{0,2,1:T(8,128)(2,1)}) %all-gather.17.cloned.1.call-update) | async-done | bytes 4194320 | tf_op jit(solution)/shard_map/all_gather | solution.py:125
  137.4 7.7 reshape.309
  145.1 9.9 copy.108
  155.0 58.2 %all-gather.19.cloned.1.call-done = bf16[4096,8,64]{0,2,1:T(8,128)(2,1)} async-done(((bf16[512,8,64]{0,2,1:T(8,128)(2,1)}), bf16[4096,8,64]{0,2,1:T(8,128)(2,1)}) %all-gather.19.cloned.1.call-update) | async-done | bytes 4194320 | tf_op jit(solution)/shard_map/all_gather | solution.py:124
  213.2 7.7 reshape.312
  220.9 9.9 copy.110
  230.8 4.3 broadcast.401.clone.1.clone
  235.1 38.7 %while.2 = (s32[]{:T(128)}, bf16[4096,8,64]{2,1,0:T(8,128)(2,1)}, s32[4,3]{1,0:T(4,128)S(1)}, bf16[4,2048,8,64]{1,3,2,0:T(8,128)(2,1)}, s32[]{:T(128)}) while((s32[]{:T(128)}, bf16[4096,8,64]{2,1,0:T(8,128)(2,1)}, s32[4,3]{1,0:T(4,128)S(1)}, bf16[4,2048,8,64]{1,3,2,0:T(8,128)(2,1)}, s32[]{:T(128)}) %tuple.122), condition=%wide.while_cond, body=%wide.while_body.sunk | while | flops 2 | bytes 12583017 | solution.py:102
  238.8 4.5 copy.173
  248.5 4.5 copy.173
  258.2 4.5 copy.173
  267.9 4.5 copy.173
  273.8 4.4 broadcast.401.clone.1.clone.1
  278.2 38.7 %while.3 = (s32[]{:T(128)}, bf16[4096,8,64]{2,1,0:T(8,128)(2,1)}, s32[4,3]{1,0:T(4,128)S(1)}, bf16[4,2048,8,64]{1,3,2,0:T(8,128)(2,1)}, s32[]{:T(128)}) while((s32[]{:T(128)}, bf16[4096,8,64]{2,1,0:T(8,128)(2,1)}, s32[4,3]{1,0:T(4,128)S(1)}, bf16[4,2048,8,64]{1,3,2,0:T(8,128)(2,1)}, s32[]{:T(128)}) %tuple.123), condition=%wide.while_cond.1, body=%wide.while_body.1.sunk | while | flops 2 | bytes 12583017 | solution.py:102
  281.9 4.5 copy.174
  291.6 4.5 copy.174
  301.3 4.5 copy.174
  311.0 4.5 copy.174
  316.9 16.6 %fusion.3 = (f32[4,128,8]{1,2,0:T(8,128)S(1)}, f32[4,8,2048,128]{3,2,1,0:T(8,128)}) fusion(pred[4,128,2048]{1,2,0:T(8,128)(4,1)S(1)} %compare_and_fusion, bf16[4,2048,8,64]{1,3,2,0:T(8,128)(2,1)} %get-tuple-element.99, bf16[4,128,8,64]{1,0,3,2:T(4,128)(2,1)} %reshape_reshape_squeeze.3), kind=kOutput, calls=%fused_computation.19 | convolution fusion | flops 1098903552 | bytes 43532288 | tf_op jit(solution)/shard_map/while/body/eval_jaxpr/sqhd,skhd->sqhk/dot_general | solution.py:132
  333.5 14.7 select_reduce_fusion
  348.2 18.7 %fusion.79 = (bf16[4,128,8,64]{1,3,2,0:T(8,128)(2,1)S(1)}, f32[4,128,8,64]{1,3,2,0:T(8,128)}) fusion(bf16[4,2048,8,64]{1,3,2,0:T(8,128)(2,1)} %get-tuple-element.78, f32[4,8,2048,128]{3,2,1,0:T(8,128)} %get-tuple-element.251, f32[4,128,8]{1,2,0:T(8,128)S(1)} %log_add_fusion, pred[4,128,2048]{1,2,0:T(8,128)(4,1)S(1)} %compare_and_fusion), kind=kOutput, calls=%fused_computation.194 | convolution fusion | flops 1115947008 | bytes 44580864 | tf_op jit(solution)/shard_map/while/body/eval_jaxpr/sqhk,skhd->sqhd/dot_general | solution.py:151
  371.2 18.1 %reduce-scatter.7.cloned.1.call-done = bf16[256,1024]{1,0:T(8,128)(2,1)} async-done(((bf16[512,1024]{1,0:T(8,128)(2,1)}), bf16[256,1024]{1,0:T(8,128)(2,1)}) %reduce-scatter.7.cloned.1.call-update) | async-done | bytes 524304 | tf_op jit(solution)/shard_map/reduce_scatter | solution.py:160
  395.0 47.2 %all-gather.25.cloned.1.call-done = bf16[1024,2048]{1,0:T(8,128)(2,1)} async-done(((bf16[64,2048]{1,0:T(8,128)(2,1)}), bf16[1024,2048]{1,0:T(8,128)(2,1)}) %all-gather.25.cloned.1.call-update) | async-done | bytes 4194320 | tf_op jit(solution)/shard_map/all_gather | solution.py:107
  442.2 22.0 %all-gather.23.cloned.1.call-done = bf16[512,1024]{1,0:T(8,128)(2,1)} async-done(((bf16[256,1024]{1,0:T(8,128)(2,1)}), bf16[512,1024]{1,0:T(8,128)(2,1)}) %all-gather.23.cloned.1.call-update) | async-done | bytes 1048592 | tf_op jit(solution)/shard_map/all_gather | solution.py:175
  464.2 15.4 %multiply_convert_fusion = (bf16[512,2048]{1,0:T(8,128)(2,1)}, f32[512,2048]{1,0:T(8,128)}, f32[512,2048]{1,0:T(8,128)}) fusion(f32[2048]{0:T(1024)S(1)} %copy-done.32, bf16[512,1024]{1,0:T(8,128)(2,1)} %all-gather.23.cloned.1.call-done, bf16[1024,2048]{1,0:T(8,128)(2,1)} %all-gather.25.cloned.1.call-done), kind=kOutput, calls=%fused_computation.38 | convolution fusion | flops 2216689664 | bytes 15736832 | tf_op jit(solution)/shard_map/dot_general | solution.py:186
  479.6 37.7 %all-gather.27.cloned.1.call-done = bf16[2048,1024]{0,1:T(8,128)(2,1)} async-done(((bf16[2048,64]{0,1:T(8,128)(2,1)}), bf16[2048,1024]{0,1:T(8,128)(2,1)}) %all-gather.27.cloned.1.call-update) | async-done | bytes 4194320 | tf_op jit(solution)/shard_map/all_gather | solution.py:108
  517.3 6.2 convolution_convert_fusion.5
  523.5 18.9 %reduce-scatter.9.cloned.1.call-done = bf16[256,1024]{1,0:T(8,128)(2,1)} async-done(((bf16[512,1024]{1,0:T(8,128)(2,1)}), bf16[256,1024]{1,0:T(8,128)(2,1)}) %reduce-scatter.9.cloned.1.call-update) | async-done | bytes 524304 | tf_op jit(solution)/shard_map/reduce_scatter | solution.py:190
  546.5 4.2 all-gather.3
  550.9 17.1 %all-gather.31.cloned.1.call-done = bf16[512,1024]{1,0:T(8,128)(2,1)} async-done(((bf16[256,1024]{1,0:T(8,128)(2,1)}), bf16[512,1024]{1,0:T(8,128)(2,1)}) %all-gather.31.cloned.1.call-update) | async-done | bytes 1048592 | tf_op jit(solution)/shard_map/all_gather | solution.py:205
  573.3 7.5 convert_reduce_fusion
  594.0 4.2 all-gather.2
  598.2 35.5 %all-reduce.7.cloned.1.call-done = bf16[512,1024]{1,0:T(8,128)(2,1)} async-done(((bf16[512,1024]{1,0:T(8,128)(2,1)}), bf16[512,1024]{1,0:T(8,128)(2,1)}) %all-reduce.7.cloned.1.call-update) | async-done | bytes 1048592 | tf_op jit(solution)/shard_map/psum | solution.py:224
  633.7 3.9 fusion.29
  642.0 19.8 %convolution_bitcast_fusion = f32[4,2048,1,8,64]{1,4,3,0,2:T(8,128)} fusion(bf16[4,128,8,64]{1,3,2,0:T(8,128)(2,1)S(1)} %copy.119, f32[4,8,2048,128]{3,2,1,0:T(8,128)} %get-tuple-element.251, f32[4,128,8]{1,2,0:T(8,128)S(1)} %log_add_fusion, pred[4,128,2048]{1,2,0:T(8,128)(4,1)S(1)} %compare_and_fusion), kind=kOutput, calls=%fused_computation.33 | convolution fusion | flops 1115684864 | bytes 51920896 | tf_op jit(solution)/shard_map/while/body/eval_jaxpr/sqhk,sqhd->skhd/dot_general | solution.py:295
  662.0 23.5 %fusion.1 = bf16[4,128,8,2048]{1,3,2,0:T(8,128)(2,1)} fusion(f32[4,8,2048,128]{3,2,1,0:T(8,128)} %get-tuple-element.251, bf16[4,2048,8,64]{1,3,2,0:T(8,128)(2,1)} %get-tuple-element.78, bf16[4,128,8,64]{1,3,2,0:T(8,128)(2,1)S(1)} %copy.119, f32[4,128,8]{1,2,0:T(8,128)S(1)} %multiply_reduce_fusion.1, f32[4,128,8]{1,2,0:T(8,128)S(1)} %log_add_fusion, ...), kind=kOutput, calls=%fused_computation.14 | convolution fusion | flops 1132462080 | bytes 60325888 | tf_op jit(solution)/shard_map/while/body/eval_jaxpr/sqhd,skhd->sqhk/dot_general | solution.py:261
  685.4 12.7 multiply_bitcast_fusion
  698.1 5.9 fusion.8
  704.1 7.8 broadcast_in_dim.125
  711.9 39.5 %dynamic_update_slice.24 = f32[4096,2,8,64]{0,3,2,1:T(8,128)} dynamic-update-slice(f32[4096,2,8,64]{0,3,2,1:T(8,128)} %broadcast_in_dim.125, f32[2048,2,8,64]{0,3,2,1:T(8,128)} %fusion.8, s32[]{:T(128)S(6)} %select_n.125, s32[]{:T(128)} %constant.87.clone.1, s32[]{:T(128)} %constant.87.clone.1, s32[]{:T(128)} %constant.87.clone.1) | dynamic-update-slice | bytes 16777220 | tf_op jit(solution)/shard_map/while/body/eval_jaxpr/dynamic_update_slice | solution.py:301
  751.4 9.8 fusion.11
  761.2 39.5 %dynamic_update_slice.25 = f32[4096,2,8,64]{0,3,2,1:T(8,128)} dynamic-update-slice(f32[4096,2,8,64]{0,3,2,1:T(8,128)} %dynamic_update_slice.24, f32[2048,2,8,64]{0,3,2,1:T(8,128)} %fusion.11, s32[]{:T(128)S(6)} %select_n.126, s32[]{:T(128)} %constant.87.clone.1, s32[]{:T(128)} %constant.87.clone.1, s32[]{:T(128)} %constant.87.clone.1) | dynamic-update-slice | bytes 16777220 | tf_op jit(solution)/shard_map/while/body/eval_jaxpr/dynamic_update_slice | solution.py:301
  800.7 9.6 fusion.6
  810.3 38.5 %dynamic_update_slice.26 = f32[4096,2,8,64]{0,3,2,1:T(8,128)} dynamic-update-slice(f32[4096,2,8,64]{0,3,2,1:T(8,128)} %dynamic_update_slice.25, f32[2048,2,8,64]{0,3,2,1:T(8,128)} %fusion.6, s32[]{:T(128)S(6)} %select_n.127, s32[]{:T(128)} %constant.87.clone.1, s32[]{:T(128)} %constant.87.clone.1, s32[]{:T(128)} %constant.87.clone.1) | dynamic-update-slice | bytes 16777220 | tf_op jit(solution)/shard_map/while/body/eval_jaxpr/dynamic_update_slice | solution.py:301
  848.9 9.4 fusion.13
  858.3 38.5 %dynamic_update_slice.27 = f32[4096,2,8,64]{0,3,2,1:T(8,128)} dynamic-update-slice(f32[4096,2,8,64]{0,3,2,1:T(8,128)} %dynamic_update_slice.26, f32[2048,2,8,64]{0,3,2,1:T(8,128)} %fusion.13, s32[]{:T(128)S(6)} %select_n.128, s32[]{:T(128)} %constant.87.clone.1, s32[]{:T(128)} %constant.87.clone.1, s32[]{:T(128)} %constant.87.clone.1) | dynamic-update-slice | bytes 16777220 | tf_op jit(solution)/shard_map/while/body/eval_jaxpr/dynamic_update_slice | solution.py:301
  896.9 9.0 convert_element_type.219
  905.9 9.4 copy.154
  915.3 9.0 copy.170
  924.3 14.4 convert_element_type.222
  942.3 6.2 convolution_convert_fusion
  949.7 5.9 convolution_convert_fusion.1
  955.9 11.3 fusion.32
  968.1 120.3 %reduce-scatter.11.cloned.1.call-done = bf16[512,2,8,64]{0,3,2,1:T(8,128)(2,1)} async-done(((bf16[4096,2,8,64]{0,3,2,1:T(8,128)(2,1)}), bf16[512,2,8,64]{0,3,2,1:T(8,128)(2,1)}) %reduce-scatter.11.cloned.1.call-update) | async-done | bytes 1048592 | tf_op jit(solution)/shard_map/reduce_scatter | solution.py:312
  1090.6 5.0 bitcast_convert_fusion
  1095.7 5.2 convert_bitcast_fusion
  1100.9 7.6 copy.135
  1110.3 60.8 %reduce-scatter.13.cloned.1.call-done = bf16[512,64]{0,1:T(8,128)(2,1)} async-done(((bf16[512,1024]{0,1:T(8,128)(2,1)}), bf16[512,64]{0,1:T(8,128)(2,1)}) %reduce-scatter.13.cloned.1.call-update) | async-done | bytes 65552 | tf_op jit(solution)/shard_map/reduce_scatter | solution.py:340
  1172.6 74.2 %reduce-scatter.17.cloned.1.call-done = bf16[2048,64]{0,1:T(8,128)(2,1)} async-done(((bf16[2048,1024]{0,1:T(8,128)(2,1)}), bf16[2048,64]{0,1:T(8,128)(2,1)}) %reduce-scatter.17.cloned.1.call-update) | async-done | bytes 262160 | tf_op jit(solution)/shard_map/reduce_scatter | solution.py:349
  1248.5 73.3 %reduce-scatter.15.cloned.1.call-done = bf16[64,2048]{1,0:T(8,128)(2,1)} async-done(((bf16[1024,2048]{1,0:T(8,128)(2,1)}), bf16[64,2048]{1,0:T(8,128)(2,1)}) %reduce-scatter.15.cloned.1.call-update) | async-done | bytes 262160 | tf_op jit(solution)/shard_map/reduce_scatter | solution.py:346
  1324.9 59.4 %all-reduce.2 = (f32[512]{0:T(512)}, f32[512]{0:T(512)}, f32[1024]{0:T(1024)}, f32[1024]{0:T(1024)}, f32[1024]{0:T(1024)}, /*index=5*/f32[2048]{0:T(1024)}, f32[1024]{0:T(1024)}, f32[1024]{0:T(1024)}, f32[1024]{0:T(1024)}) all-reduce(f32[512]{0:T(512)S(1)} %convert_reduce_fusion.5, ...), channel_id=1, replica_groups=mesh['fsdp'=2,'context'=8,'tensor'=2] {'fsdp','context'}, use_global_device_ids=true, to_apply=%region_24.25 | all-reduce | flops 9216 | bytes 73728 | tf_op jit(solution)/shard_map/psum | solution.py:353
  1387.1 92.1 %all-reduce.11.cloned.1.call-done = bf16[1024,3,512]{2,1,0:T(4,128)(2,1)} async-done(((bf16[1024,3,512]{2,1,0:T(4,128)(2,1)}), bf16[1024,3,512]{2,1,0:T(4,128)(2,1)}) %all-reduce.11.cloned.1.call-update) | async-done | bytes 3145744
  (215 shorter events, 101.9 us)
Async XLA Ops:
  7.2 51.0 %all-gather.15.cloned.1.call-start = ((), (), s32[]{:S(2)}) async-start(), calls=%async_computation.6 | async-start | bytes 3342336 | tf_op jit(solution)/shard_map/all_gather | solution.py:105
  7.9 129.5 %all-gather.17.cloned.1.call-start = ((), (), s32[]{:S(2)}) async-start(), calls=%async_computation.7 | async-start | bytes 4718592 | tf_op jit(solution)/shard_map/all_gather | solution.py:125
  62.3 3.0 copy-start.33
  62.3 3.9 copy-start.34
  63.4 149.9 %all-gather.19.cloned.1.call-start = ((), (), s32[]{:S(2)}) async-start(), calls=%async_computation.8 | async-start | bytes 4718592 | tf_op jit(solution)/shard_map/all_gather | solution.py:124
  64.1 303.3 %all-gather.21.cloned.1.call-start = ((), (), s32[]{:S(2)}) async-start(), calls=%async_computation.9 | async-start | bytes 1114112 | tf_op jit(solution)/shard_map/all_gather | solution.py:106
  64.7 324.6 %reduce-scatter.7.cloned.1.call-start = ((), (), s32[]{:S(2)}) async-start(), calls=%async_computation.10 | async-start | bytes 1572864 | tf_op jit(solution)/shard_map/reduce_scatter | solution.py:160
  66.2 78.9 %copy-start.17 = (s32[4]{0:T(128)}, s32[4]{0:T(128)S(1)}, u32[]{:S(2)}) copy-start(s32[4]{0:T(128)S(1)} %broadcast_minimum_fusion) | copy-start | bytes 52
  366.9 22.4 %copy-start.6 = (bf16[512,1024]{1,0:T(8,128)(2,1)S(1)}, bf16[512,1024]{1,0:T(8,128)(2,1)}, u32[]{:S(2)}) copy-start(bf16[512,1024]{1,0:T(8,128)(2,1)} %param.17) | copy-start | bytes 3145732
  366.9 22.4 %copy-start.14 = (f32[1024]{0:T(1024)S(1)}, f32[1024]{0:T(1024)}, u32[]{:S(2)}) copy-start(f32[1024]{0:T(1024)} %param.24) | copy-start | bytes 12292
  366.9 25.1 %copy-start.16 = (f32[1024]{0:T(1024)S(1)}, f32[1024]{0:T(1024)}, u32[]{:S(2)}) copy-start(f32[1024]{0:T(1024)} %param.25) | copy-start | bytes 12292
  366.9 25.1 %copy-start.19 = (f32[1024]{0:T(1024)S(1)}, f32[1024]{0:T(1024)}, u32[]{:S(2)}) copy-start(f32[1024]{0:T(1024)} %param.26) | copy-start | bytes 12292
  367.4 26.8 %copy-start.8 = (bf16[4,128,8,64]{1,0,3,2:T(4,128)(2,1)}, bf16[4,128,8,64]{1,0,3,2:T(4,128)(2,1)S(1)}, u32[]{:S(2)}) copy-start(bf16[4,128,8,64]{1,0,3,2:T(4,128)(2,1)S(1)} %copy.116) | copy-start | bytes 1572868
  367.4 96.8 %copy-start.32 = (f32[2048]{0:T(1024)S(1)}, f32[2048]{0:T(1024)}, u32[]{:S(2)}) copy-start(f32[2048]{0:T(1024)} %param.28) | copy-start | bytes 24580
  370.6 71.6 %all-gather.25.cloned.1.call-start = ((), (), s32[]{:S(2)}) async-start(), calls=%async_computation.12 | async-start | bytes 4456448 | tf_op jit(solution)/shard_map/all_gather | solution.py:107
  371.1 93.1 %all-gather.23.cloned.1.call-start = ((), (), s32[]{:S(2)}) async-start(), calls=%async_computation.11 | async-start | bytes 1572864 | tf_op jit(solution)/shard_map/all_gather | solution.py:175
  394.2 123.1 %all-gather.27.cloned.1.call-start = ((), (), s32[]{:S(2)}) async-start(), calls=%async_computation.13 | async-start | bytes 4456448 | tf_op jit(solution)/shard_map/all_gather | solution.py:108
  394.9 147.5 %reduce-scatter.9.cloned.1.call-start = ((), (), s32[]{:S(2)}) async-start(), calls=%async_computation.14 | async-start | bytes 1572864 | tf_op jit(solution)/shard_map/reduce_scatter | solution.py:190
  517.3 25.2 %copy-start.4 = (bf16[256,1024]{1,0:T(8,128)(2,1)S(1)}, bf16[256,1024]{1,0:T(8,128)(2,1)}, u32[]{:S(2)}) copy-start(bf16[256,1024]{1,0:T(8,128)(2,1)} %reduce-scatter.7.cloned.1.call-done) | copy-start | bytes 1572868
  517.3 25.2 %copy-start.27 = (f32[1024]{0:T(1024)S(1)}, f32[1024]{0:T(1024)}, u32[]{:S(2)}) copy-start(f32[1024]{0:T(1024)} %param.30) | copy-start | bytes 12292
  523.5 21.7 %copy-start.15 = (f32[1024]{0:T(1024)S(1)}, f32[1024]{0:T(1024)}, u32[]{:S(2)}) copy-start(f32[1024]{0:T(1024)} %param.31) | copy-start | bytes 12292
  523.5 21.7 %copy-start.28 = (f32[1024]{0:T(1024)S(1)}, f32[1024]{0:T(1024)}, u32[]{:S(2)}) copy-start(f32[1024]{0:T(1024)} %param.32) | copy-start | bytes 12292
  523.5 44.5 %copy-start.2 = (bf16[512,1024]{1,0:T(8,128)(2,1)S(1)}, bf16[512,1024]{1,0:T(8,128)(2,1)}, u32[]{:S(2)}) copy-start(bf16[512,1024]{1,0:T(8,128)(2,1)} %param.33) | copy-start | bytes 3145732
  523.5 44.5 %all-gather.31.cloned.1.call-start = ((), (), s32[]{:S(2)}) async-start(), calls=%async_computation.16 | async-start | bytes 1572864 | tf_op jit(solution)/shard_map/all_gather | solution.py:205
  546.5 51.7 %all-gather.33.cloned.1.call-start = ((), (), s32[]{:S(2)}) async-start(), calls=%async_computation.18 | async-start | bytes 1572864 | tf_op jit(solution)/shard_map/all_gather | solution.py:178
  550.8 82.8 %all-reduce.7.cloned.1.call-start = ((), (), s32[]{:S(2)}) async-start(), calls=%async_computation.17 | async-start | bytes 2097152 | tf_op jit(solution)/shard_map/psum | solution.py:224
  568.0 5.3 copy-start.30
  573.3 7.5 copy-start.12
  573.3 8.9 copy-start.29
  580.8 1.4 copy-start.36
  582.1 3.4 copy-start.18
  582.2 51.5 %copy-start.3 = (bf16[512,1024]{1,0:T(8,128)(2,1)S(1)}, bf16[512,1024]{1,0:T(8,128)(2,1)}, u32[]{:S(2)}) copy-start(bf16[512,1024]{1,0:T(8,128)(2,1)} %all-gather.31.cloned.1.call-done) | copy-start | bytes 3145732
  585.5 502.8 %reduce-scatter.11.cloned.1.call-start = ((), (), s32[]{:S(2)}) async-start(), calls=%async_computation.19 | async-start | bytes 9437184 | tf_op jit(solution)/shard_map/reduce_scatter | solution.py:312
  633.7 3.9 copy-start.7
  637.6 2.5 copy-start.10
  638.8 1.3 copy-start
  642.0 19.8 %copy-start.11 = (f32[4,128,8,64]{1,3,2,0:T(8,128)S(1)}, f32[4,128,8,64]{1,3,2,0:T(8,128)}, u32[]{:S(2)}) copy-start(f32[4,128,8,64]{1,3,2,0:T(8,128)} %get-tuple-element.253) | copy-start | bytes 3145732
  662.0 23.5 %copy-start.5 = (bf16[4,128,8,64]{1,0,3,2:T(4,128)(2,1)S(1)}, bf16[4,128,8,64]{1,0,3,2:T(4,128)(2,1)}, u32[]{:S(2)}) copy-start(bf16[4,128,8,64]{1,0,3,2:T(4,128)(2,1)} %reshape_reshape_squeeze.3) | copy-start | bytes 1572868
  938.7 1.6 copy-start.1
  938.7 1.7 copy-start.9
  938.8 171.3 %all-gather.29.cloned.1.call-start = ((), (), s32[]{:S(2)}) async-start(), calls=%async_computation.15 | async-start | bytes 1572864 | tf_op jit(solution)/shard_map/all_gather | solution.py:202
  939.3 231.7 %reduce-scatter.13.cloned.1.call-start = ((), (), s32[]{:S(2)}) async-start(), calls=%async_computation.21 | async-start | bytes 1114112 | tf_op jit(solution)/shard_map/reduce_scatter | solution.py:340
  942.2 304.5 %reduce-scatter.17.cloned.1.call-start = ((), (), s32[]{:S(2)}) async-start(), calls=%async_computation.23 | async-start | bytes 4456448 | tf_op jit(solution)/shard_map/reduce_scatter | solution.py:349
  948.5 1.2 copy-start.31
  948.5 373.3 %reduce-scatter.15.cloned.1.call-start = ((), (), s32[]{:S(2)}) async-start(), calls=%async_computation.22 | async-start | bytes 4456448 | tf_op jit(solution)/shard_map/reduce_scatter | solution.py:346
  955.6 428.6 %all-reduce.9.cloned.1.call-start = ((), (), s32[]{:S(2)}) async-start(), calls=%async_computation.20 | async-start | bytes 2097152 | tf_op jit(solution)/shard_map/psum | solution.py:330
  1095.7 383.5 %all-reduce.11.cloned.1.call-start = ((), (), s32[]{:S(2)}) async-start(), calls=%async_computation.24 | async-start | bytes 8388608
  1100.9 7.7 copy-start.35
  1108.5 216.3 %copy-start.20 = (f32[1024]{0:T(1024)S(1)}, f32[1024]{0:T(1024)}, u32[]{:S(2)}) copy-start(f32[1024]{0:T(1024)} %get-tuple-element.195) | copy-start | bytes 12292
  1108.5 216.3 %copy-start.21 = (f32[1024]{0:T(1024)S(1)}, f32[1024]{0:T(1024)}, u32[]{:S(2)}) copy-start(f32[1024]{0:T(1024)} %get-tuple-element.199) | copy-start | bytes 12292
  1108.5 216.3 %copy-start.22 = (f32[1024]{0:T(1024)S(1)}, f32[1024]{0:T(1024)}, u32[]{:S(2)}) copy-start(f32[1024]{0:T(1024)} %get-tuple-element.225) | copy-start | bytes 12292
  1108.5 216.3 %copy-start.23 = (f32[1024]{0:T(1024)S(1)}, f32[1024]{0:T(1024)}, u32[]{:S(2)}) copy-start(f32[1024]{0:T(1024)} %get-tuple-element.192) | copy-start | bytes 12292
  1108.5 216.3 %copy-start.24 = (f32[1024]{0:T(1024)S(1)}, f32[1024]{0:T(1024)}, u32[]{:S(2)}) copy-start(f32[1024]{0:T(1024)} %get-tuple-element.197) | copy-start | bytes 12292
  1108.5 216.3 %copy-start.25 = (f32[1024]{0:T(1024)S(1)}, f32[1024]{0:T(1024)}, u32[]{:S(2)}) copy-start(f32[1024]{0:T(1024)} %get-tuple-element.229) | copy-start | bytes 12292
  1108.5 216.3 %copy-start.26 = (f32[2048]{0:T(1024)S(1)}, f32[2048]{0:T(1024)}, u32[]{:S(2)}) copy-start(f32[2048]{0:T(1024)} %get-tuple-element.227) | copy-start | bytes 24580
  1248.5 232.5 %copy-start.13 = (bf16[512,1024]{1,0:T(8,128)(2,1)S(1)}, bf16[512,1024]{1,0:T(8,128)(2,1)}, u32[]{:S(2)}) copy-start(bf16[512,1024]{1,0:T(8,128)(2,1)} %all-gather.29.cloned.1.call-done) | copy-start | bytes 3145732
Sparse Core Ops, SparseCore 0:
  10.2 47.8 all-gather.14
  63.5 73.8 all-gather.16
  140.0 73.1 all-gather.18
  215.3 36.1 all-gather.20
  370.7 18.5 reduce-scatter.6
  391.6 50.5 all-gather.24
  444.4 19.7 all-gather.22
  466.7 50.5 all-gather.26
  523.6 18.7 reduce-scatter.8
  546.6 21.3 all-gather.30
  570.1 21.2 all-gather.32
  593.6 40.0 all-reduce.6
  938.9 149.4 reduce-scatter.10
  1089.8 20.3 all-gather.28
  1113.6 57.4 reduce-scatter.12
  1175.3 71.4 reduce-scatter.16
  1250.4 71.3 reduce-scatter.14
  1324.6 39.1 all-reduce.8
  1367.5 111.6 all-reduce.10
where the time goes:
time: 1500 us; the launch traced here: 1490 us
  waiting for transfers between devices  796 us (53%)
  local copies, waits for them, and re-layouts  341 us (23%)
  matrix products  167 us (11%)
  other arithmetic  93.1 us (6%)
  blocking collectives  67.9 us (5%)
  between operations  23.2 us (2%)
    dynamic_update_slice x4, local copies, waits for them, and re-layouts, back_step(): lax.dynamic_update_slice_in_dim(key_terms, earlier + terms[index], begins...  156 us
    reduce_scatter x1, waiting for transfers between devices, per_device(): lax.psum_scatter(jnp.swapaxes(key_terms.reshape((slots, contexts, BLK) +...  120 us
    unnamed x20, waiting for transfers between devices  95.9 us
    gather x32, local copies, waits for them, and re-layouts  77.4 us
    reduce_scatter x1, waiting for transfers between devices, per_device(): lax.psum_scatter(grad_w_down.astype(jnp.bfloat16), ('fsdp', 'context'), s...  74.2 us
    reduce_scatter x1, waiting for transfers between devices, per_device(): lax.psum_scatter(grad_w_up.astype(jnp.bfloat16), ('fsdp', 'context'), sca...  73.3 us
    all_gather x1, waiting for transfers between devices, per_device(): lax.all_gather(value_low, 'context', axis=0, tiled=True)  66.7 us
    reduce_scatter x1, waiting for transfers between devices, per_device(): lax.psum_scatter(grad_w_attn_out.astype(jnp.bfloat16), ('fsdp', 'context'...  60.8 us
  transfers between devices with their start and end apart: 19, of which 16 were waited for; matrix products, arithmetic and copies ran while one was open for 18% of the time, Pallas kernels for 0%

commit v1 on v0

--- a/solution.py
+++ b/solution.py
@@ -1,6 +1,10 @@
+import functools
+
 import jax
 import jax.numpy as jnp
 from jax import lax
+from jax.experimental import pallas as pl
+from jax.experimental.pallas import tpu as pltpu
 from jax.sharding import PartitionSpec as P
 
 HEAD = 64
@@ -383,6 +387,671 @@
     )
 
 
+MESH = pl.DeviceIdType.MESH
+CHUNK = 512
+VMEM_LIMIT = 48 * 1024 * 1024
+
+
+def ring_place(context, depth):
+    z, x = context // 2, context % 2
+    return z + x * (2 * depth - 1 - 2 * z)
+
+
+def ring_context(place, depth):
+    x = place // depth
+    z = place + x * (2 * depth - 1 - 2 * place)
+    return 2 * z + x
+
+
+def ring_facts(contexts):
+    depth = contexts // 2
+    fsdp, context = lax.axis_index("fsdp"), lax.axis_index("context")
+    place = ring_place(context, depth)
+
+    def at(offset):
+        return ring_context((place + offset + 2 * contexts) % contexts, depth)
+
+    return fsdp, context, at
+
+
+def greet(targets):
+    barrier = pltpu.get_barrier_semaphore()
+    for target in targets:
+        pl.semaphore_signal(barrier, inc=1, device_id=target, device_id_type=MESH)
+    pl.semaphore_wait(barrier, len(targets))
+
+
+def gather_kernel(contexts, count, *refs):
+    shards, fulls = refs[:count], refs[count : 2 * count]
+    local_sem, send_sem, recv_sem, pair_send, pair_recv = refs[2 * count :]
+    fsdp, context, at = ring_facts(contexts)
+    half = shards[0].shape[0] // 2
+    toward = ({"context": at(1)}, {"context": at(-1)})
+    pair = {"fsdp": 1 - fsdp}
+    greet([toward[0], toward[1], pair])
+
+    def own(index):
+        return pltpu.make_async_copy(
+            shards[index], fulls[index].at[fsdp * contexts + context], local_sem.at[index]
+        )
+
+    def piece(index, way, step):
+        block = fsdp * contexts + at(-step if way == 0 else step)
+        return fulls[index].at[block, pl.ds(way * half, half)]
+
+    def hop(index, way, step):
+        ref = piece(index, way, step)
+        return pltpu.make_async_remote_copy(
+            src_ref=ref,
+            dst_ref=ref,
+            send_sem=send_sem.at[step, index, way],
+            recv_sem=recv_sem.at[step, index, way],
+            device_id=toward[way],
+            device_id_type=MESH,
+        )
+
+    def arrival(index, way, step):
+        ref = piece(index, way, step + 1)
+        return pltpu.make_async_remote_copy(
+            src_ref=ref,
+            dst_ref=ref,
+            send_sem=send_sem.at[step, index, way],
+            recv_sem=recv_sem.at[step, index, way],
+            device_id=toward[way],
+            device_id_type=MESH,
+        )
+
+    def across(index, way, step):
+        ref = piece(index, way, step)
+        return pltpu.make_async_remote_copy(
+            src_ref=ref,
+            dst_ref=ref,
+            send_sem=pair_send.at[step, index, way],
+            recv_sem=pair_recv.at[step, index, way],
+            device_id=pair,
+            device_id_type=MESH,
+        )
+
+    def across_arrival(index, way, step):
+        block = (1 - fsdp) * contexts + at(-step if way == 0 else step)
+        ref = fulls[index].at[block, pl.ds(way * half, half)]
+        return pltpu.make_async_remote_copy(
+            src_ref=ref,
+            dst_ref=ref,
+            send_sem=pair_send.at[step, index, way],
+            recv_sem=pair_recv.at[step, index, way],
+            device_id=pair,
+            device_id_type=MESH,
+        )
+
+    for index in range(count):
+        own(index).start()
+    for index in range(count):
+        own(index).wait()
+        for way in range(2):
+            hop(index, way, 0).start()
+            across(index, way, 0).start()
+
+    def onward(step, carry):
+        for index in range(count):
+            for way in range(2):
+                arrival(index, way, step - 1).wait_recv()
+                hop(index, way, step).start()
+                across(index, way, step).start()
+        return carry
+
+    lax.fori_loop(1, contexts - 1, onward, 0)
+    for index in range(count):
+        for way in range(2):
+            arrival(index, way, contexts - 2).wait_recv()
+            across(index, way, contexts - 1).start()
+
+    def finish(step, carry):
+        for index in range(count):
+            for way in range(2):
+                across(index, way, step).wait_send()
+                across_arrival(index, way, step).wait_recv()
+        return carry
+
+    def finish_hop(step, carry):
+        for index in range(count):
+            for way in range(2):
+                hop(index, way, step).wait_send()
+        return carry
+
+    lax.fori_loop(0, contexts - 1, finish_hop, 0)
+    lax.fori_loop(0, contexts, finish, 0)
+
+
+def gather_rows(shards, contexts, collective_id):
+    count = len(shards)
+    fulls = pl.pallas_call(
+        functools.partial(gather_kernel, contexts, count),
+        out_shape=[
+            jax.ShapeDtypeStruct((2 * contexts,) + shard.shape, shard.dtype) for shard in shards
+        ],
+        in_specs=[pl.BlockSpec(memory_space=pl.ANY)] * count,
+        out_specs=[pl.BlockSpec(memory_space=pl.ANY)] * count,
+        scratch_shapes=[
+            pltpu.SemaphoreType.DMA((count,)),
+            pltpu.SemaphoreType.DMA((contexts - 1, count, 2)),
+            pltpu.SemaphoreType.DMA((contexts - 1, count, 2)),
+            pltpu.SemaphoreType.DMA((contexts, count, 2)),
+            pltpu.SemaphoreType.DMA((contexts, count, 2)),
+        ],
+        compiler_params=pltpu.CompilerParams(collective_id=collective_id, has_side_effects=True),
+        name="gather_rows",
+    )(*shards)
+    return [full.reshape(-1, full.shape[-1]) for full in fulls]
+
+
+def scatter_kernel(contexts, count, *refs):
+    grads, small = refs[:count], refs[count]
+    outs, small_out = refs[count + 1 : 2 * count + 1], refs[2 * count + 1]
+    rest = refs[2 * count + 2 :]
+    pairs, slots, small_in = rest[:count], rest[count : 2 * count], rest[2 * count]
+    small_now = rest[2 * count + 1]
+    send_sem, recv_sem, pair_send, pair_recv, small_send, small_recv = rest[2 * count + 2 :]
+    fsdp, context, at = ring_facts(contexts)
+    half = outs[0].shape[0] // 2
+    toward = ({"context": at(1)}, {"context": at(-1)})
+    pair = {"fsdp": 1 - fsdp}
+    steps = []
+    width = 1
+    while width < contexts:
+        steps.append({"context": context + width - 2 * width * ((context // width) % 2)})
+        width *= 2
+    partners = [pair] + steps
+    greet([toward[0], toward[1]] + partners)
+
+    def rows(way):
+        return pl.ds(way * half, half)
+
+    def block_at(way, step):
+        return at(-1 - step if way == 0 else 1 + step)
+
+    def across(index, way, step):
+        block = block_at(way, step)
+        return pltpu.make_async_remote_copy(
+            src_ref=grads[index].at[1 - fsdp, block, rows(way)],
+            dst_ref=pairs[index].at[block, rows(way)],
+            send_sem=pair_send.at[step, index, way],
+            recv_sem=pair_recv.at[step, index, way],
+            device_id=pair,
+            device_id_type=MESH,
+        )
+
+    def hop(index, way, step):
+        return pltpu.make_async_remote_copy(
+            src_ref=pairs[index].at[block_at(way, step), rows(way)],
+            dst_ref=slots[index].at[step, rows(way)],
+            send_sem=send_sem.at[step, index, way],
+            recv_sem=recv_sem.at[step, index, way],
+            device_id=toward[way],
+            device_id_type=MESH,
+        )
+
+    def small_hop(step):
+        return pltpu.make_async_remote_copy(
+            src_ref=small_now.at[step],
+            dst_ref=small_in.at[step],
+            send_sem=small_send.at[step],
+            recv_sem=small_recv.at[step],
+            device_id=partners[step],
+            device_id_type=MESH,
+        )
+
+    def pair_sum(index, way, step):
+        across(index, way, step).wait_recv()
+        block = block_at(way, step)
+        return grads[index][fsdp, block, rows(way)].astype(jnp.float32) + pairs[index][
+            block, rows(way)
+        ].astype(jnp.float32)
+
+    small_now[0] = small[...]
+    small_hop(0).start()
+
+    def offer(step, carry):
+        for index in range(count):
+            for way in range(2):
+                across(index, way, step).start()
+        return carry
+
+    lax.fori_loop(0, contexts, offer, 0)
+
+    for index in range(count):
+        for way in range(2):
+            total = pair_sum(index, way, 0)
+            pairs[index][block_at(way, 0), rows(way)] = total.astype(jnp.bfloat16)
+            hop(index, way, 0).start()
+
+    for step in range(len(partners)):
+        small_hop(step).wait()
+        total = small_now[step] + small_in[step]
+        if step + 1 < len(partners):
+            small_now[step + 1] = total
+            small_hop(step + 1).start()
+        else:
+            small_out[...] = total
+
+    def onward(step, carry):
+        for index in range(count):
+            for way in range(2):
+                total = pair_sum(index, way, step)
+                hop(index, way, step - 1).wait_recv()
+                total = total + slots[index][step - 1, rows(way)].astype(jnp.float32)
+                pairs[index][block_at(way, step), rows(way)] = total.astype(jnp.bfloat16)
+                hop(index, way, step).start()
+        return carry
+
+    lax.fori_loop(1, contexts - 1, onward, 0)
+    for index in range(count):
+        for way in range(2):
+            total = pair_sum(index, way, contexts - 1)
+            hop(index, way, contexts - 2).wait_recv()
+            outs[index][rows(way)] = total + slots[index][contexts - 2, rows(way)].astype(
+                jnp.float32
+            )
+
+    def finish(step, carry):
+        for index in range(count):
+            for way in range(2):
+                across(index, way, step).wait_send()
+        return carry
+
+    def finish_hop(step, carry):
+        for index in range(count):
+            for way in range(2):
+                hop(index, way, step).wait_send()
+        return carry
+
+    lax.fori_loop(0, contexts, finish, 0)
+    lax.fori_loop(0, contexts - 1, finish_hop, 0)
+
+
+def scatter_rows(grads, small, contexts, collective_id):
+    count = len(grads)
+    rows = grads[0].shape[0] // (2 * contexts)
+    widths = [grad.shape[1] for grad in grads]
+    doubling = 1 + (contexts - 1).bit_length()
+    vmem = pl.BlockSpec(memory_space=pltpu.VMEM)
+    return pl.pallas_call(
+        functools.partial(scatter_kernel, contexts, count),
+        out_shape=[jax.ShapeDtypeStruct((rows, width), jnp.float32) for width in widths]
+        + [jax.ShapeDtypeStruct(small.shape, jnp.float32)],
+        in_specs=[vmem] * (count + 1),
+        out_specs=[vmem] * (count + 1),
+        scratch_shapes=[pltpu.VMEM((contexts, rows, width), jnp.bfloat16) for width in widths]
+        + [pltpu.VMEM((contexts - 1, rows, width), jnp.bfloat16) for width in widths]
+        + [
+            pltpu.VMEM((doubling,) + small.shape, jnp.float32),
+            pltpu.VMEM((doubling,) + small.shape, jnp.float32),
+            pltpu.SemaphoreType.DMA((contexts - 1, count, 2)),
+            pltpu.SemaphoreType.DMA((contexts - 1, count, 2)),
+            pltpu.SemaphoreType.DMA((contexts, count, 2)),
+            pltpu.SemaphoreType.DMA((contexts, count, 2)),
+            pltpu.SemaphoreType.DMA((doubling,)),
+            pltpu.SemaphoreType.DMA((doubling,)),
+        ],
+        compiler_params=pltpu.CompilerParams(
+            collective_id=collective_id, has_side_effects=True, vmem_limit_bytes=VMEM_LIMIT
+        ),
+        name="scatter_rows",
+    )(*[grad.reshape(2, contexts, rows, grad.shape[1]) for grad in grads], small)
+
+
+def swap_kernel(contexts, to_heads, source, result, local_sem, send_sem, recv_sem):
+    context = lax.axis_index("context")
+    others = [(context + shift) % contexts for shift in range(1, contexts)]
+    greet([{"context": other} for other in others])
+
+    def ends(there):
+        if to_heads:
+            return source.at[there], result.at[:, context]
+        return source.at[:, there], result.at[context]
+
+    here, mine = ends(context)
+    keep = pltpu.make_async_copy(here, mine, local_sem)
+    copies = []
+    for index, other in enumerate(others):
+        sent, landed = ends(other)
+        copies.append(
+            pltpu.make_async_remote_copy(
+                src_ref=sent,
+                dst_ref=landed,
+                send_sem=send_sem.at[index],
+                recv_sem=recv_sem.at[index],
+                device_id={"context": other},
+                device_id_type=MESH,
+            )
+        )
+    for copy in copies:
+        copy.start()
+    keep.start()
+    keep.wait()
+    for copy in copies:
+        copy.wait()
+
+
+def swap(source, contexts, to_heads, collective_id):
+    shape = (source.shape[1], source.shape[0]) + source.shape[2:]
+    return pl.pallas_call(
+        functools.partial(swap_kernel, contexts, to_heads),
+        out_shape=jax.ShapeDtypeStruct(shape, source.dtype),
+        in_specs=[pl.BlockSpec(memory_space=pl.ANY)],
+        out_specs=pl.BlockSpec(memory_space=pl.ANY),
+        scratch_shapes=[
+            pltpu.SemaphoreType.DMA(()),
+            pltpu.SemaphoreType.DMA((contexts - 1,)),
+            pltpu.SemaphoreType.DMA((contexts - 1,)),
+        ],
+        compiler_params=pltpu.CompilerParams(collective_id=collective_id, has_side_effects=True),
+        name="swap_heads" if to_heads else "swap_rows",
+    )(source)
+
+
+def turned(block):
+    return block.astype(jnp.float32).T.astype(jnp.bfloat16)
+
+
+def key_mask(scores, first_key, low, high):
+    keys = first_key + lax.broadcasted_iota(jnp.int32, scores.shape, 0)
+    return jnp.where((keys >= low) & (keys < high), scores, MASKED)
+
+
+def attend_kernel(meta, qkv, att, att_wide, log_total, keys, values, held):
+    blocks = qkv.shape[0]
+    window = held.shape[0]
+
+    def lay(block, carry):
+        place = pl.ds(pl.multiple_of(block * BLK, BLK), BLK)
+        keys[place, :] = turned(qkv[block, HEAD : 2 * HEAD])
+        values[:, place] = qkv[block, 2 * HEAD : 3 * HEAD]
+        return carry
+
+    lax.fori_loop(0, blocks, lay, 0)
+
+    def one(block, carry):
+        begin, low, high = meta[0, block], meta[1, block], meta[2, block]
+        query = qkv[block, 0:HEAD]
+        top = jnp.full((1, BLK), MASKED, jnp.float32)
+        for part in range(0, window, CHUNK):
+            place = pl.ds(pl.multiple_of(begin + part, BLK), CHUNK)
+            scores = jnp.dot(keys[place, :], query, preferred_element_type=jnp.float32)
+            scores = key_mask(scores, begin + part, low, high)
+            held[part : part + CHUNK] = scores
+            top = jnp.maximum(top, jnp.max(scores, axis=0, keepdims=True))
+        total = jnp.zeros((1, BLK), jnp.float32)
+        out = jnp.zeros((HEAD, BLK), jnp.float32)
+        for part in range(0, window, CHUNK):
+            place = pl.ds(pl.multiple_of(begin + part, BLK), CHUNK)
+            prob = jnp.exp(held[part : part + CHUNK] - top)
+            total += jnp.sum(prob, axis=0, keepdims=True)
+            out += jnp.dot(
+                values[:, place], prob.astype(jnp.bfloat16), preferred_element_type=jnp.float32
+            )
+        out = out / total
+        att_wide[block] = out
+        att[block] = out.astype(jnp.bfloat16)
+        log_total[block] = top + jnp.log(total)
+        return carry
+
+    lax.fori_loop(0, blocks, one, 0)
+
+
+def attend(meta, qkv):
+    blocks = qkv.shape[0]
+    rows = blocks * BLK
+    vmem = pl.BlockSpec(memory_space=pltpu.VMEM)
+    return pl.pallas_call(
+        attend_kernel,
+        out_shape=[
+            jax.ShapeDtypeStruct((blocks, HEAD, BLK), jnp.bfloat16),
+            jax.ShapeDtypeStruct((blocks, HEAD, BLK), jnp.float32),
+            jax.ShapeDtypeStruct((blocks, 1, BLK), jnp.float32),
+        ],
+        in_specs=[pl.BlockSpec(memory_space=pltpu.SMEM), vmem],
+        out_specs=[vmem] * 3,
+        scratch_shapes=[
+            pltpu.VMEM((rows, HEAD), jnp.bfloat16),
+            pltpu.VMEM((HEAD, rows), jnp.bfloat16),
+            pltpu.VMEM((MAXB * BLK, BLK), jnp.float32),
+        ],
+        compiler_params=pltpu.CompilerParams(vmem_limit_bytes=VMEM_LIMIT),
+        name="attend",
+    )(meta, qkv)
+
+
+def attend_back_kernel(
+    meta, qkv, grad_att, att_wide, log_total, grads, keys, keys_turned, values, grad_k, grad_v
+):
+    blocks = qkv.shape[0]
+    window = MAXB * BLK
+
+    def lay(block, carry):
+        place = pl.ds(pl.multiple_of(block * BLK, BLK), BLK)
+        keys[place, :] = turned(qkv[block, HEAD : 2 * HEAD])
+        keys_turned[:, place] = qkv[block, HEAD : 2 * HEAD]
+        values[place, :] = turned(qkv[block, 2 * HEAD : 3 * HEAD])
+        grad_k[place, :] = jnp.zeros((BLK, HEAD), jnp.float32)
+        grad_v[place, :] = jnp.zeros((BLK, HEAD), jnp.float32)
+        return carry
+
+    lax.fori_loop(0, blocks, lay, 0)
+
+    def one(block, carry):
+        begin, low, high = meta[0, block], meta[1, block], meta[2, block]
+        query = qkv[block, 0:HEAD]
+        grad = grad_att[block]
+        query_rows = turned(query)
+        grad_rows = turned(grad)
+        delta = jnp.sum(grad.astype(jnp.float32) * att_wide[block], axis=0, keepdims=True)
+        log_row = log_total[block]
+        grad_q = jnp.zeros((HEAD, BLK), jnp.float32)
+        for part in range(0, window, CHUNK):
+            place = pl.ds(pl.multiple_of(begin + part, BLK), CHUNK)
+            scores = jnp.dot(keys[place, :], query, preferred_element_type=jnp.float32)
+            prob = jnp.exp(key_mask(scores, begin + part, low, high) - log_row)
+            grad_prob = jnp.dot(values[place, :], grad, preferred_element_type=jnp.float32)
+            grad_score = (prob * (grad_prob - delta)).astype(jnp.bfloat16)
+            grad_q += jnp.dot(
+                keys_turned[:, place], grad_score, preferred_element_type=jnp.float32
+            )
+            grad_k[place, :] += jnp.dot(grad_score, query_rows, preferred_element_type=jnp.float32)
+            grad_v[place, :] += jnp.dot(
+                prob.astype(jnp.bfloat16), grad_rows, preferred_element_type=jnp.float32
+            )
+        grads[block, 0:HEAD] = (grad_q * HEAD ** (-0.5)).astype(jnp.bfloat16)
+        return carry
+
+    lax.fori_loop(0, blocks, one, 0)
+
+    def store(block, carry):
+        place = pl.ds(pl.multiple_of(block * BLK, BLK), BLK)
+        grads[block, HEAD : 2 * HEAD] = grad_k[place, :].T.astype(jnp.bfloat16)
+        grads[block, 2 * HEAD : 3 * HEAD] = grad_v[place, :].T.astype(jnp.bfloat16)
+        return carry
+
+    lax.fori_loop(0, blocks, store, 0)
+
+
+def attend_back(meta, qkv, grad_att, att_wide, log_total):
+    blocks = qkv.shape[0]
+    rows = blocks * BLK
+    vmem = pl.BlockSpec(memory_space=pltpu.VMEM)
+    return pl.pallas_call(
+        attend_back_kernel,
+        out_shape=jax.ShapeDtypeStruct(qkv.shape, jnp.bfloat16),
+        in_specs=[pl.BlockSpec(memory_space=pltpu.SMEM)] + [vmem] * 4,
+        out_specs=vmem,
+        scratch_shapes=[
+            pltpu.VMEM((rows, HEAD), jnp.bfloat16),
+            pltpu.VMEM((HEAD, rows), jnp.bfloat16),
+            pltpu.VMEM((rows, HEAD), jnp.bfloat16),
+            pltpu.VMEM((rows, HEAD), jnp.float32),
+            pltpu.VMEM((rows, HEAD), jnp.float32),
+        ],
+        compiler_params=pltpu.CompilerParams(vmem_limit_bytes=VMEM_LIMIT),
+        name="attend_back",
+    )(meta, qkv, grad_att, att_wide, log_total)
+
+
+def over_tensor(low):
+    other = lax.ppermute(low, "tensor", [(0, 1), (1, 0)])
+    return low.astype(jnp.float32) + other.astype(jnp.float32)
+
+
+def ring_device(
+    tokens,
+    doc_blocks,
+    pad_tokens,
+    w_qkv,
+    bias_query,
+    bias_value,
+    w_attn_out,
+    bias_attn_out,
+    gain_one,
+    shift_one,
+    w_up,
+    bias_up,
+    w_down,
+    bias_down,
+    gain_two,
+    shift_two,
+    cotangent,
+):
+    contexts = lax.axis_size("context")
+    row_count, width = tokens.shape
+    slots = row_count // BLK
+    inner_width = w_qkv.shape[2]
+    heads_here = inner_width // HEAD
+    blocks = slots * contexts
+    wide = functools.partial(jnp.einsum, preferred_element_type=jnp.float32)
+
+    doc_ends = jnp.cumsum(doc_blocks[0]) * BLK
+    firsts = jnp.arange(blocks, dtype=jnp.int32) * BLK
+    doc_of_block = jnp.sum((firsts[:, None] >= doc_ends[None, :]).astype(jnp.int32), axis=1)
+    chosen = doc_of_block[:, None] == jnp.arange(doc_ends.shape[0], dtype=jnp.int32)[None, :]
+    low = jnp.sum(jnp.where(chosen, doc_ends - doc_blocks[0] * BLK, 0), axis=1)
+    high = jnp.sum(jnp.where(chosen, doc_ends - pad_tokens[0], 0), axis=1)
+    begin = jnp.minimum(low, (blocks - MAXB) * BLK)
+    meta = jnp.stack([begin, low, high]).astype(jnp.int32)
+
+    full_qkv, full_out, full_up, full_down = gather_rows(
+        [w_qkv.reshape(w_qkv.shape[0], -1), w_attn_out.T, w_up, w_down.T], contexts, 0
+    )
+
+    bias_three = jnp.concatenate([bias_query, jnp.zeros_like(bias_query), bias_value])
+    qkv = (wide("td,df->tf", tokens, full_qkv) + bias_three).astype(jnp.bfloat16)
+    query_scale = jnp.concatenate(
+        [jnp.full((inner_width,), HEAD ** (-0.5)), jnp.ones((2 * inner_width,))]
+    ).astype(jnp.bfloat16)
+    qkv_heads = (
+        (qkv * query_scale)
+        .reshape(slots, BLK, 3, heads_here, HEAD)
+        .transpose(3, 0, 2, 4, 1)
+        .reshape(heads_here, slots, 3 * HEAD, BLK)
+    )
+    qkv_here = swap(qkv_heads, contexts, True, 1).reshape(blocks, 3 * HEAD, BLK)
+    att_low, att_wide, log_total = attend(meta, qkv_here)
+    att_back = swap(att_low.reshape(slots, contexts, HEAD, BLK), contexts, False, 2)
+    attended_low = att_back.transpose(1, 3, 0, 2).reshape(row_count, inner_width)
+
+    branch = (
+        over_tensor(wide("te,de->td", attended_low, full_out).astype(jnp.bfloat16)) + bias_attn_out
+    )
+    first, normed_one, factor_one = layer_norm(
+        tokens.astype(jnp.float32) + branch, gain_one, shift_one
+    )
+    first_low = first.astype(jnp.bfloat16)
+    pre = wide("td,df->tf", first_low, full_up) + bias_up
+    act, gelu_back = jax.vjp(lambda hidden: jax.nn.gelu(hidden, approximate=False), pre)
+    act_low = act.astype(jnp.bfloat16)
+    feed = over_tensor(wide("tf,df->td", act_low, full_down).astype(jnp.bfloat16)) + bias_down
+    out, normed_two, factor_two = layer_norm(first + feed, gain_two, shift_two)
+    output = out.astype(jnp.bfloat16)
+
+    grad_out = cotangent.astype(jnp.float32)
+    grad_gain_two = jnp.sum(grad_out * normed_two, axis=0)
+    grad_shift_two = jnp.sum(grad_out, axis=0)
+    grad_second = norm_back(grad_out, normed_two, factor_two, gain_two)
+    grad_feed = grad_second.astype(jnp.bfloat16)
+    grad_bias_down = jnp.sum(grad_feed.astype(jnp.float32), axis=0)
+    grad_act = wide("td,df->tf", grad_feed, full_down)
+    grad_pre = gelu_back(grad_act)[0].astype(jnp.bfloat16)
+    grad_bias_up = jnp.sum(grad_pre.astype(jnp.float32), axis=0)
+    grad_first = grad_second + over_tensor(
+        wide("tf,df->td", grad_pre, full_up).astype(jnp.bfloat16)
+    )
+    grad_w_down = wide("td,tf->df", grad_feed, act_low).astype(jnp.bfloat16)
+    grad_w_up = wide("td,tf->df", first_low, grad_pre).astype(jnp.bfloat16)
+    grad_gain_one = jnp.sum(grad_first * normed_one, axis=0)
+    grad_shift_one = jnp.sum(grad_first, axis=0)
+    grad_mid = norm_back(grad_first, normed_one, factor_one, gain_one)
+    grad_branch = grad_mid.astype(jnp.bfloat16)
+    grad_bias_attn_out = jnp.sum(grad_branch.astype(jnp.float32), axis=0)
+    grad_w_attn_out = wide("td,te->de", grad_branch, attended_low).astype(jnp.bfloat16)
+    grad_att = (
+        wide("td,de->te", grad_branch, full_out)
+        .astype(jnp.bfloat16)
+        .reshape(slots, BLK, heads_here, HEAD)
+        .transpose(2, 0, 3, 1)
+    )
+    grad_att_here = swap(grad_att, contexts, True, 3).reshape(blocks, HEAD, BLK)
+    grad_here = attend_back(meta, qkv_here, grad_att_here, att_wide, log_total)
+    grad_qkv = (
+        swap(grad_here.reshape(slots, contexts, 3 * HEAD, BLK), contexts, False, 4)
+        .reshape(heads_here, slots, 3, HEAD, BLK)
+        .transpose(1, 4, 2, 0, 3)
+        .reshape(row_count, 3 * inner_width)
+    )
+    grad_bias = jnp.sum(grad_qkv.astype(jnp.float32), axis=0)
+    grad_tokens = grad_mid + over_tensor(
+        wide("tf,df->td", grad_qkv, full_qkv).astype(jnp.bfloat16)
+    )
+    grad_w_qkv = wide("td,tf->df", tokens, grad_qkv).astype(jnp.bfloat16)
+    smalls = [
+        grad_bias[:inner_width],
+        grad_bias[2 * inner_width :],
+        grad_bias_attn_out,
+        grad_gain_one,
+        grad_shift_one,
+        grad_bias_up,
+        grad_bias_down,
+        grad_gain_two,
+        grad_shift_two,
+    ]
+    shard_qkv, shard_out, shard_up, shard_down, small_rows = scatter_rows(
+        [grad_w_qkv, grad_w_attn_out, grad_w_up, grad_w_down],
+        jnp.concatenate(smalls).reshape(-1, 128),
+        contexts,
+        5,
+    )
+    flat = small_rows.reshape(-1)
+    sums = []
+    start = 0
+    for small in smalls:
+        sums.append(flat[start : start + small.shape[0]])
+        start += small.shape[0]
+    return (
+        output,
+        grad_tokens,
+        shard_qkv.reshape(w_qkv.shape),
+        sums[0],
+        sums[1],
+        shard_out.T,
+        sums[2],
+        sums[3],
+        sums[4],
+        shard_up,
+        sums[5],
+        shard_down.T,
+        sums[6],
+        sums[7],
+        sums[8],
+    )
+
+
 def solution(mesh):
     in_specs = (
         P(("fsdp", "context"), None),
@@ -420,6 +1089,14 @@
         P(),
         P(),
     )
+    contexts = mesh.shape["context"]
+    heads_each = 1024 // HEAD // mesh.shape["tensor"]
+    fits = (
+        mesh.shape["fsdp"] == 2
+        and mesh.shape["tensor"] == 2
+        and contexts == 8
+        and heads_each == contexts
+    )
     return jax.shard_map(
-        per_device, mesh=mesh, in_specs=in_specs, out_specs=out_specs, check_vma=False
-    )
+        ring_device if fits else per_device, mesh=mesh, in_specs=in_specs, out_specs=out_specs, check_vma=False
+    )

time: 1500 us -> 506 us (0.34)
  waiting for transfers between devices: 796 us -> 60.7 us
  Pallas kernels: 0 us -> 345 us
  local copies, waits for them, and re-layouts: 341 us -> 26.7 us
  matrix products: 167 us -> 44.3 us
  other arithmetic: 93.1 us -> 17.9 us
  blocking collectives: 67.9 us -> 0 us
  between operations: 23.2 us -> 1.64 us
    reduce_scatter x6 -> x0, waiting for transfers between devices: 366 us -> none  [the longest x1 120 us: per_device(): lax.psum_scatter(jnp.swapaxes(key_terms.reshape((slots, contexts, BLK) +...]
    pallas_call x0 -> x8, Pallas kernels: none -> 345 us  [the longest x4 95.1 us: swap(): pl.pallas_call(functools.partial(swap_kernel, contexts, to_heads), out_sh...]
    all_gather x10 -> x0, waiting for transfers between devices: 299 us -> none  [the longest x1 66.7 us: per_device(): lax.all_gather(value_low, 'context', axis=0, tiled=True)]
    dynamic_update_slice x4 -> x0, local copies, waits for them, and re-layouts: 156 us -> none  [back_step(): lax.dynamic_update_slice_in_dim(key_terms, earlier + terms[index], begins...]
    dot_general x18 -> x12, matrix products: 167 us -> 44.3 us  [the longest x1 13.2 us: ring_device(): pre = wide('td,df->tf', first_low, full_up) + bias_up]
    unnamed x20 -> x0, waiting for transfers between devices: 95.9 us -> none
    gather x32 -> x0, local copies, waits for them, and re-layouts: 77.4 us -> none
    ppermute x0 -> x4, waiting for transfers between devices: none -> 60.7 us  [over_tensor(): other = lax.ppermute(low, 'tensor', [(0, 1), (1, 0)])]
  transfers between devices with their start and end apart: 19 -> 4, of which waited for: 16 -> 3; matrix products, arithmetic and copies ran while one was open for 18% -> 3% of each run, Pallas kernels for 0% -> 18%
where the time goes in v1:
time: 506 us; the launch traced here: 498 us
  Pallas kernels  345 us (68%)
  waiting for transfers between devices  60.7 us (12%)
  matrix products  44.3 us (9%)
  local copies, waits for them, and re-layouts  26.7 us (5%)
  other arithmetic  17.9 us (4%)
    pallas_call x4, Pallas kernels, swap(): pl.pallas_call(functools.partial(swap_kernel, contexts, to_heads), out_sh...  95.1 us
    pallas_call x1, Pallas kernels, scatter_rows(): pl.pallas_call(functools.partial(scatter_kernel, contexts, count), out_sh...  87.7 us
    pallas_call x1, Pallas kernels, gather_rows(): pl.pallas_call(functools.partial(gather_kernel, contexts, count), out_sha...  87.2 us
    ppermute x4, waiting for transfers between devices, over_tensor(): other = lax.ppermute(low, 'tensor', [(0, 1), (1, 0)])  60.7 us
    pallas_call x1, Pallas kernels, attend_back(): pl.pallas_call(attend_back_kernel, out_shape=jax.ShapeDtypeStruct(qkv.sha...  48 us
    pallas_call x1, Pallas kernels, attend(): pl.pallas_call(attend_kernel, out_shape=[jax.ShapeDtypeStruct((blocks, HE...  27 us
    dot_general x1, matrix products, ring_device(): pre = wide('td,df->tf', first_low, full_up) + bias_up  13.2 us
    unnamed x75, local copies, waits for them, and re-layouts  13.1 us
  transfers between devices with their start and end apart: 4, of which 3 were waited for; matrix products, arithmetic and copies ran while one was open for 3% of the time, Pallas kernels for 18%

profile of v1, /device:TPU:0, one launch (start us, length us, event | category | flops | bytes accessed | tf_op | source)
XLA Modules:
  0.0 498.4 jit_solution(10522154484122804904)
XLA Ops:
  0.7 0.8 reduce-window.7
  1.5 0.7 bitcast_subtract_fusion
  2.3 1.6 copy.52
  4.0 0.7 pad_maximum_fusion
  4.7 87.2 %gather_rows.1 = (bf16[16,64,1536]{2,1,0:T(8,128)(2,1)}, bf16[16,64,512]{2,1,0:T(8,128)(2,1)}, bf16[16,64,2048]{2,1,0:T(8,128)(2,1)}, bf16[16,64,2048]{2,1,0:T(8,128)(2,1)}) custom-call(bf16[64,1536]{1,0:T(8,128)(2,1)} %bitcast.127, bf16[64,512]{1,0:T(8,128)(2,1)} %bitcast.131, bf16[64,2048]{1,0:T(8,128)(2,1)} %refs_2_.1, bf16[64,2048]{1,0:T(8,128)(2,1)} %bitcast.129), custom_call_target="tpu_custom_call" | custom-call | tf_op jit(solution)/shard_map/gather_rows/pallas_call | solution.py:528
  91.9 4.4 fusion.11
  96.3 0.4 reshape.193
  96.7 1.6 copy.43
  98.3 29.7 %swap_heads.2 = bf16[4,8,192,128]{3,2,1,0:T(8,128)(2,1)} custom-call(bf16[8,4,192,128]{3,2,1,0:T(8,128)(2,1)} %bitcast.116), custom_call_target="tpu_custom_call" | custom-call | tf_op jit(solution)/shard_map/swap_heads/pallas_call | solution.py:738
  128.1 1.4 copy-done
  129.5 27.0 %attend.1 = (bf16[32,64,128]{2,1,0:T(8,128)(2,1)S(1)}, f32[32,64,128]{2,1,0:T(8,128)S(1)}, f32[32,1,128]{2,1,0:T(1,128)S(1)}) custom-call(s32[3,32]{1,0:T(4,128)S(1)} %pad_add_fusion.meta, bf16[32,192,128]{2,1,0:T(8,128)(2,1)S(1)} %bitcast.103), custom_call_target="tpu_custom_call" | custom-call | tf_op jit(solution)/shard_map/attend/pallas_call | solution.py:806
  156.5 1.0 copy-done.4
  157.5 0.8 copy-done.6
  158.3 21.5 %swap_rows.2 = bf16[8,4,64,128]{3,2,1,0:T(8,128)(2,1)} custom-call(bf16[4,8,64,128]{3,2,1,0:T(8,128)(2,1)} %bitcast.110), custom_call_target="tpu_custom_call" | custom-call | tf_op jit(solution)/shard_map/swap_rows/pallas_call | solution.py:738
  179.9 1.5 copy.44
  181.4 0.8 convolution_convert_fusion.4
  182.2 1.4 collective-permute-start
  183.6 23.3 %collective-permute-done = bf16[512,1024]{1,0:T(8,128)(2,1)S(1)} collective-permute-done((bf16[512,1024]{1,0:T(8,128)(2,1)S(1)}, bf16[512,1024]{1,0:T(8,128)(2,1)S(1)}, u32[]{:S(2)}, u32[]{:S(2)}) %collective-permute-start) | collective-permute-done | bytes 1048608 | tf_op jit(solution)/shard_map/ppermute | solution.py:900
  206.9 0.6 fusion.42
  207.5 0.3 multiply_reduce_fusion.3
  207.9 1.2 copy-done.23
  209.1 13.2 %multiply_convert_fusion = (bf16[512,2048]{1,0:T(8,128)(2,1)S(1)}, f32[512,2048]{1,0:T(8,128)}, f32[512,2048]{1,0:T(8,128)}) fusion(f32[2048]{0:T(1024)S(1)} %copy-done.27, bf16[1024,2048]{1,0:T(8,128)(2,1)S(1)} %bitcast.135, f32[512,1024]{1,0:T(8,128)S(1)} %get-tuple-element.104, f32[1024]{0:T(1024)S(1)} %copy-done.22, f32[1024]{0:T(1024)S(1)} %copy-done.17, ...), kind=kOutput, calls=%fused_computation.4 | convolution fusion | flops 2219311104 | bytes 16797696 | tf_op jit(solution)/shard_map/td,df->tf/dot_general | solution.py:967
  222.4 3.3 convolution_convert_fusion.6
  225.7 0.3 collective-permute-start.1
  226.0 23.8 %collective-permute-done.1 = bf16[512,1024]{1,0:T(8,128)(2,1)} collective-permute-done((bf16[512,1024]{1,0:T(8,128)(2,1)}, bf16[512,1024]{1,0:T(8,128)(2,1)}, u32[]{:S(2)}, u32[]{:S(2)}) %collective-permute-start.1) | collective-permute-done | bytes 1048608 | tf_op jit(solution)/shard_map/ppermute | solution.py:900
  249.8 2.6 fusion.40
  252.4 0.3 multiply_reduce_fusion.2
  252.8 0.8 copy-done.10
  253.6 1.0 fusion.15
  254.6 1.8 convert_reduce_fusion.3
  256.5 1.2 copy-done.26
  257.7 4.1 convert_reduce_fusion
  261.8 2.4 convolution_convert_fusion.5
  264.2 0.3 collective-permute-start.2
  264.6 4.4 convolution_convert_fusion
  268.9 4.5 convolution_convert_fusion.1
  273.5 13.6 %collective-permute-done.2 = bf16[512,1024]{1,0:T(8,128)(2,1)S(1)} collective-permute-done((bf16[512,1024]{1,0:T(8,128)(2,1)S(1)}, bf16[512,1024]{1,0:T(8,128)(2,1)S(1)}, u32[]{:S(2)}, u32[]{:S(2)}) %collective-permute-start.2) | collective-permute-done | bytes 1048608 | tf_op jit(solution)/shard_map/ppermute | solution.py:900
  287.1 1.3 multiply_reduce_fusion
  288.4 0.7 convert_reduce_fusion.4
  289.1 0.5 copy-done.14
  289.7 0.7 convolution_convert_fusion.7
  290.4 0.2 copy-done.12
  290.6 0.8 convolution_convert_fusion.3
  291.4 1.6 reshape.212
  293.0 2.7 copy.46
  295.7 14.5 %swap_heads.3 = bf16[4,8,64,128]{3,2,1,0:T(8,128)(2,1)} custom-call(bf16[8,4,64,128]{3,2,1,0:T(8,128)(2,1)} %bitcast.121), custom_call_target="tpu_custom_call" | custom-call | tf_op jit(solution)/shard_map/swap_heads/pallas_call | solution.py:738
  310.2 1.0 copy-done.3
  311.3 1.2 copy-done.5
  312.5 48.0 %attend_back.1 = bf16[32,192,128]{2,1,0:T(8,128)(2,1)S(1)} custom-call(s32[3,32]{1,0:T(4,128)S(1)} %pad_add_fusion.meta, bf16[32,192,128]{2,1,0:T(8,128)(2,1)S(1)} %bitcast.104, bf16[32,64,128]{2,1,0:T(8,128)(2,1)S(1)} %bitcast.108, f32[32,64,128]{2,1,0:T(8,128)S(1)} %copy-done.5, f32[32,1,128]{2,1,0:T(1,128)S(1)} %get-tuple-element.33.log_total), custom_call_target="tpu_custom_call" | custom-call | tf_op jit(solution)/shard_map/attend_back/pallas_call | solution.py:882
  360.6 1.2 copy-done.2
  361.8 29.3 %swap_rows.3 = bf16[8,4,192,128]{3,2,1,0:T(8,128)(2,1)} custom-call(bf16[4,8,192,128]{3,2,1,0:T(8,128)(2,1)} %bitcast.105), custom_call_target="tpu_custom_call" | custom-call | tf_op jit(solution)/shard_map/swap_rows/pallas_call | solution.py:738
  391.1 5.0 %convert_reduce_fusion.1 = f32[3,8,64]{2,1,0:T(8,128)S(1)} fusion(bf16[8,4,3,64,128]{4,3,2,1,0:T(8,128)(2,1)} %bitcast.114), kind=kLoop, calls=%fused_computation.22 | loop fusion | flops 1571328 | bytes 1579008 | tf_op jit(solution)/shard_map/reduce_sum | solution.py:1008
  396.1 1.4 copy.47
  397.7 3.8 fusion.20
  401.7 1.8 convolution_convert_fusion.2
  403.6 87.7 %scatter_rows.1 = (f32[64,1536]{1,0:T(8,128)S(1)}, f32[64,512]{1,0:T(8,128)S(1)}, f32[64,2048]{1,0:T(8,128)S(1)}, f32[64,2048]{1,0:T(8,128)S(1)}, f32[72,128]{1,0:T(8,128)S(1)}) custom-call(bf16[2,8,64,1536]{3,2,1,0:T(8,128)(2,1)S(1)} %bitcast.107, bf16[2,8,64,512]{3,2,1,0:T(8,128)(2,1)S(1)} %bitcast.106, bf16[2,8,64,2048]{3,2,1,0:T(8,128)(2,1)} %bitcast.118, ...), custom_call_target="tpu_custom_call" | custom-call | tf_op jit(solution)/shard_map/scatter_rows/pallas_call | solution.py:678
  491.3 0.8 copy.73
  492.1 0.6 slice_bitcast_fusion.7
  492.7 0.6 slice_bitcast_fusion
  493.3 0.6 slice_bitcast_fusion.1
  493.9 1.8 add_add_fusion
  495.7 0.7 copy.86
  496.3 0.8 copy.87
  497.1 0.8 copy.88
  (82 shorter events, 0.7 us)
Async XLA Ops:
  98.3 83.1 %copy-start.13 = (bf16[16,64,512]{2,1,0:T(8,128)(2,1)S(1)}, bf16[16,64,512]{2,1,0:T(8,128)(2,1)}, u32[]{:S(2)}) copy-start(bf16[16,64,512]{2,1,0:T(8,128)(2,1)} %get-tuple-element.29) | copy-start | bytes 3145732
  128.0 1.4 copy-start
  156.5 1.0 copy-start.4
  157.5 0.8 copy-start.6
  179.8 27.1 %copy-start.15 = (bf16[512,1024]{1,0:T(8,128)(2,1)S(1)}, bf16[512,1024]{1,0:T(8,128)(2,1)}, u32[]{:S(2)}) copy-start(bf16[512,1024]{1,0:T(8,128)(2,1)} %param.17) | copy-start | bytes 3145732
  179.8 27.1 %copy-start.19 = (f32[1024]{0:T(1024)S(1)}, f32[1024]{0:T(1024)}, u32[]{:S(2)}) copy-start(f32[1024]{0:T(1024)} %param.24) | copy-start | bytes 12292
  181.4 2.2 copy-start.11
  182.2 24.7 %collective-permute-start = (bf16[512,1024]{1,0:T(8,128)(2,1)S(1)}, bf16[512,1024]{1,0:T(8,128)(2,1)S(1)}, u32[]{:S(2)}, u32[]{:S(2)}) collective-permute-start(bf16[512,1024]{1,0:T(8,128)(2,1)S(1)} %convolution_convert_fusion.4), channel_id=1, source_target_pairs={{0,1},{1,0},{2,3},{3,2},{4,5},{5,4},{6,7},{7,6},{8,9},{9,8},{10,11... | collective-permute-start | bytes 3145736 | tf_op jit(solution)/shard_map/ppermute | solution.py:900
  206.9 2.2 copy-start.23
  207.5 1.6 copy-start.17
  207.5 1.6 copy-start.22
  207.5 1.6 copy-start.27
  209.1 13.3 %copy-start.25 = (bf16[16,64,2048]{2,1,0:T(8,128)(2,1)S(1)}, bf16[16,64,2048]{2,1,0:T(8,128)(2,1)}, u32[]{:S(2)}) copy-start(bf16[16,64,2048]{2,1,0:T(8,128)(2,1)} %get-tuple-element.31) | copy-start | bytes 12582916
  222.4 3.4 copy-start.28
  222.4 27.4 %copy-start.20 = (f32[1024]{0:T(1024)S(1)}, f32[1024]{0:T(1024)}, u32[]{:S(2)}) copy-start(f32[1024]{0:T(1024)} %param.30) | copy-start | bytes 12292
  225.7 24.1 %collective-permute-start.1 = (bf16[512,1024]{1,0:T(8,128)(2,1)}, bf16[512,1024]{1,0:T(8,128)(2,1)}, u32[]{:S(2)}, u32[]{:S(2)}) collective-permute-start(bf16[512,1024]{1,0:T(8,128)(2,1)} %convolution_convert_fusion.6), channel_id=1, source_target_pairs={{0,1},{1,0},{2,3},{3,2},{4,5},{5,4},{6,7},{7,6},{8,9},{9,8},{10,11... | collective-permute-start | bytes 3145736 | tf_op jit(solution)/shard_map/ppermute | solution.py:900
  249.8 6.7 %copy-start.31 = (f32[512,2048]{1,0:T(8,128)S(1)}, f32[512,2048]{1,0:T(8,128)}, u32[]{:S(2)}) copy-start(f32[512,2048]{1,0:T(8,128)} %get-tuple-element.118) | copy-start | bytes 12582916
  252.4 1.2 copy-start.10
  252.4 1.2 copy-start.18
  252.8 1.9 copy-start.21
  253.6 2.9 copy-start.30
  254.6 3.1 copy-start.26
  257.7 4.1 copy-start.24
  261.8 2.8 copy-start.29
  264.2 22.9 %collective-permute-start.2 = (bf16[512,1024]{1,0:T(8,128)(2,1)S(1)}, bf16[512,1024]{1,0:T(8,128)(2,1)S(1)}, u32[]{:S(2)}, u32[]{:S(2)}) collective-permute-start(bf16[512,1024]{1,0:T(8,128)(2,1)S(1)} %convolution_convert_fusion.5), channel_id=1, source_target_pairs={{0,1},{1,0},{2,3},{3,2},{4,5},{5,4},{6,7},{7,6},{8,9},{9,8},{10,11... | collective-permute-start | bytes 3145736 | tf_op jit(solution)/shard_map/ppermute | solution.py:900
  288.4 1.2 copy-start.14
  289.1 1.3 copy-start.7
  289.1 1.5 copy-start.12
  291.4 18.8 %copy-start.1 = (bf16[4,8,192,128]{3,2,1,0:T(8,128)(2,1)S(1)}, bf16[4,8,192,128]{3,2,1,0:T(8,128)(2,1)}, u32[]{:S(2)}) copy-start(bf16[4,8,192,128]{3,2,1,0:T(8,128)(2,1)} %swap_heads.2) | copy-start | bytes 4718596
  310.2 1.0 copy-start.3
  311.3 1.2 copy-start.5
  360.5 1.2 copy-start.2
  391.0 5.0 %copy-start.9 = (bf16[8,4,192,128]{3,2,1,0:T(8,128)(2,1)S(1)}, bf16[8,4,192,128]{3,2,1,0:T(8,128)(2,1)}, u32[]{:S(2)}) copy-start(bf16[8,4,192,128]{3,2,1,0:T(8,128)(2,1)} %swap_rows.3) | copy-start | bytes 4718596
  397.7 4.0 copy-start.16
  401.5 92.4 %collective-permute-start.3 = (bf16[512,1024]{1,0:T(8,128)(2,1)S(1)}, bf16[512,1024]{1,0:T(8,128)(2,1)S(1)}, u32[]{:S(2)}, u32[]{:S(2)}) collective-permute-start(bf16[512,1024]{1,0:T(8,128)(2,1)S(1)} %fusion.20), channel_id=1, source_target_pairs={{0,1},{1,0},{2,3},{3,2},{4,5},{5,4},{6,7},{7,6},{8,9},{9,8},{10,11... | collective-permute-start | bytes 3145736 | tf_op jit(solution)/shard_map/ppermute | solution.py:900
  403.6 90.3 %copy-start.8 = (f32[512,1024]{1,0:T(8,128)S(1)}, f32[512,1024]{1,0:T(8,128)}, u32[]{:S(2)}) copy-start(f32[512,1024]{1,0:T(8,128)} %copy-done.7) | copy-start | bytes 6291460
